TPU v7x, 32 devices: a whole 2x2x4 slice. The times are simulated.
32 devices in a mesh: chan: 8 (over z, y), hour: 4 (over x, core).
Axes of the slice: x: 2, y: 2, z: 4, core: 2. Of those that a mesh axis runs over, the one named last changes fastest.
Arguments:
- records: bfloat16 [320, 64, 2048], P('chan', 'hour'), may hold values from -6 to 6
- live_channels: int32 [320], P('chan'), may hold values 0 or 1
- live_windows: int32 [64], P('hour'), may hold values 0 or 1
Outputs:
- correlations: bfloat16 [320, 2, 40, 512], P('chan', None, None, 'hour')
All inputs are finite; a program needn't handle non-finite values. No bound on the sum of `live_channels` or of `live_windows` on one device may be relied on, other than what follows from the above.
Results may differ from a plain program's by a relative error of at most 0.013.
Values may be sent and summed in bfloat16 or wider, within the bound.
A program may use at most 128 MiB of HBM per device.

v0:
```python
import functools
import math

import jax
import jax.numpy as jnp
import ml_dtypes
import numpy as np
from jax import lax
from jax.experimental import pallas as pl
from jax.experimental.pallas import tpu as pltpu
from jax.sharding import PartitionSpec as P

SAMPLES = 2048
BAND = 512
FIRST_BIN = 32
HALF = 64
LAGS = 512
NSHIFT = 2
GROUP = 8
LANES = 128
MESH = pl.DeviceIdType.MESH


def forward_table():
    times = np.arange(SAMPLES)[:, None]
    bins = FIRST_BIN + np.arange(BAND)[None, :]
    angle = (times * bins % SAMPLES) * (2.0 * math.pi / SAMPLES)
    return np.concatenate([np.cos(angle), -np.sin(angle)], axis=1).astype(ml_dtypes.bfloat16)


def inverse_table():
    bins = FIRST_BIN + np.arange(BAND)[:, None]
    shifts = np.arange(LAGS)[None, :] - LAGS // 2
    angle = (bins * shifts % SAMPLES) * (2.0 * math.pi / SAMPLES)
    return np.concatenate([np.cos(angle), -np.sin(angle)], axis=0).astype(ml_dtypes.bfloat16)


def band_inside():
    index = np.arange(BAND)
    return np.abs(index[:, None] - index[None, :]) <= HALF


def kernel(
    n_chan, n_hour, channels, windows, norm_factor,
    records, live, forward, inside, weight, inverse, out,
    own, own_send, far_two, far_one, cross, lagged, heard, total,
    two_send, two_recv, one_send, one_recv, sum_send, sum_recv,
):
    chunks = channels // GROUP
    rows = GROUP * windows
    quarter = LAGS // n_hour
    me = lax.axis_index("chan")
    hour = lax.axis_index("hour")
    parity = lax.rem(me, 2)
    before = lax.rem(me + n_chan - 2, n_chan)
    after = lax.rem(me + 2, n_chan)
    twin = me + 1 - 2 * parity

    barrier = pltpu.get_barrier_semaphore()
    for chan in (before, after, twin):
        pl.semaphore_signal(barrier, inc=1, device_id=(chan, hour), device_id_type=MESH)
    for step in range(1, n_hour):
        other = lax.rem(hour + step, n_hour)
        pl.semaphore_signal(barrier, inc=1, device_id=(me, other), device_id_type=MESH)
    pl.semaphore_wait(barrier, 3 + n_hour - 1)

    def to_before(chunk):
        return pltpu.make_async_remote_copy(
            src_ref=own_send.at[chunk], dst_ref=far_two.at[chunk],
            send_sem=two_send.at[chunk], recv_sem=two_recv.at[chunk],
            device_id=(before, hour), device_id_type=MESH,
        )

    def to_twin(source, chunk):
        return pltpu.make_async_remote_copy(
            src_ref=source.at[chunk], dst_ref=far_one.at[chunk],
            send_sem=one_send.at[chunk], recv_sem=one_recv.at[chunk],
            device_id=(twin, hour), device_id_type=MESH,
        )

    def to_hour(step, distance):
        target = lax.rem(hour + distance, n_hour)
        return pltpu.make_async_remote_copy(
            src_ref=lagged.at[step, target], dst_ref=heard.at[step, distance - 1],
            send_sem=sum_send.at[step, distance - 1], recv_sem=sum_recv.at[step, distance - 1],
            device_id=(me, target), device_id_type=MESH,
        )

    def whiten_chunk(chunk, carry):
        start = pl.multiple_of(chunk * rows, rows)
        spectra = jnp.dot(
            records[pl.ds(start, rows), :], forward[...], preferred_element_type=jnp.float32
        )
        real_part = spectra[:, :BAND]
        imag_part = spectra[:, BAND:]
        amplitude = jnp.sqrt(real_part * real_part + imag_part * imag_part)
        high = amplitude.astype(jnp.bfloat16)
        low = (amplitude - high.astype(jnp.float32)).astype(jnp.bfloat16)
        smooth = jnp.dot(high, inside[...], preferred_element_type=jnp.float32)
        smooth = smooth + jnp.dot(low, inside[...], preferred_element_type=jnp.float32)
        factor = live[pl.ds(start, rows), :] / (smooth * weight[...] + 1e-06)
        for tile in range(BAND // LANES):
            at = slice(tile * LANES, (tile + 1) * LANES)
            for half, part in enumerate((real_part, imag_part)):
                value = (part[:, at] * factor[:, at]).astype(jnp.bfloat16).astype(jnp.float32)
                own[half * (BAND // LANES) + tile, pl.ds(start, rows), :] = value
        for tile in range(2 * BAND // LANES):
            for pair in range(windows // 2):
                both = [
                    own[tile, pl.ds(start + 2 * pair + part, GROUP, stride=windows), :]
                    for part in range(2)
                ]
                own_send[chunk, pl.ds(pair * 2 * GROUP, 2 * GROUP), pl.ds(tile * LANES, LANES)] = (
                    jnp.concatenate(both, axis=0).astype(jnp.bfloat16)
                )
        to_before(chunk).start()

        @pl.when(parity == 1)
        def _():
            to_twin(own_send, chunk).start()

        return carry

    lax.fori_loop(0, chunks, whiten_chunk, 0)

    def cross_lags(far, chunk, step):
        for tile in range(BAND // LANES):
            real_at = pl.ds(tile * LANES, LANES)
            imag_at = pl.ds(BAND + tile * LANES, LANES)
            far_real, far_imag = [], []
            for pair in range(windows // 2):
                at = pl.ds(pair * 2 * GROUP, 2 * GROUP)
                for lanes, parts in ((real_at, far_real), (imag_at, far_imag)):
                    both = far[chunk, at, lanes].astype(jnp.float32)
                    parts += [both[:GROUP], both[GROUP:]]

            def channel_pair(index, carry):
                reals, imags = [], []
                for part in range(2):
                    base = pl.multiple_of((2 * index + part) * windows, windows)
                    real = jnp.zeros((GROUP, LANES), jnp.float32)
                    imag = jnp.zeros((GROUP, LANES), jnp.float32)
                    for window in range(windows):
                        a_real = own[tile, pl.ds(base + window, GROUP, stride=0), :]
                        a_imag = own[BAND // LANES + tile, pl.ds(base + window, GROUP, stride=0), :]
                        real = real + a_real * far_real[window] + a_imag * far_imag[window]
                        imag = imag + a_real * far_imag[window] - a_imag * far_real[window]
                    reals.append(real)
                    imags.append(imag)
                at = pl.ds(pl.multiple_of(index * 2 * GROUP, 2 * GROUP), 2 * GROUP)
                cross[at, real_at] = jnp.concatenate(reals, axis=0).astype(jnp.bfloat16)
                cross[at, imag_at] = jnp.concatenate(imags, axis=0).astype(jnp.bfloat16)
                return carry

            lax.fori_loop(0, channels // 2, channel_pair, 0)
        result = jnp.dot(cross[...], inverse[...], preferred_element_type=jnp.float32) * norm_factor
        for part in range(n_hour):
            lagged[step, part] = result[:, part * quarter : (part + 1) * quarter].astype(jnp.bfloat16)
        for distance in range(1, n_hour):
            to_hour(step, distance).start()

    def correlate_chunk(chunk, carry):
        to_before(chunk).wait_recv()

        @pl.when(parity == 0)
        def _():
            to_twin(far_two, chunk).start()

        cross_lags(far_two, chunk, 2 * chunk + 1)
        to_twin(own_send, chunk).wait_recv()
        cross_lags(far_one, chunk, 2 * chunk)
        return carry

    lax.fori_loop(0, chunks, correlate_chunk, 0)

    def finish_chunk(chunk, carry):
        to_before(chunk).wait_send()
        to_twin(own_send, chunk).wait_send()
        for shift in range(NSHIFT):
            step = 2 * chunk + shift
            value = lagged[step, hour].astype(jnp.float32)
            for distance in range(1, n_hour):
                to_hour(step, distance).wait()
                value = value + heard[step, distance - 1].astype(jnp.float32)
            at = pl.ds(pl.multiple_of(chunk * GROUP, GROUP), GROUP)
            total[:, shift, at, :] = value.reshape(channels, GROUP, quarter)
        return carry

    lax.fori_loop(0, chunks, finish_chunk, 0)
    out[...] = total[...].astype(jnp.bfloat16)


def local(records, live_channels, live_windows):
    channels, windows, samples = records.shape
    n_chan, n_hour = lax.axis_size("chan"), lax.axis_size("hour")
    norm_factor = 1.0 / math.sqrt(windows * n_hour * BAND)
    chunks, rows, quarter = channels // GROUP, GROUP * windows, LAGS // n_hour
    steps = NSHIFT * chunks
    live = (
        live_channels.astype(jnp.float32)[:, None] * live_windows.astype(jnp.float32)[None, :]
    ).reshape(channels * windows, 1)
    inside = band_inside()
    weight = (1.0 / inside.sum(axis=0, keepdims=True)).astype(np.float32)
    whitened = pltpu.VMEM((chunks, rows, 2 * BAND), jnp.bfloat16)
    return pl.pallas_call(
        functools.partial(kernel, n_chan, n_hour, channels, windows, norm_factor),
        out_shape=jax.ShapeDtypeStruct((channels, NSHIFT, channels, quarter), jnp.bfloat16),
        in_specs=[pl.BlockSpec(memory_space=pltpu.VMEM)] * 6,
        out_specs=pl.BlockSpec(memory_space=pltpu.VMEM),
        scratch_shapes=[
            pltpu.VMEM((2 * BAND // LANES, channels * windows, LANES), jnp.float32),
            whitened,
            whitened,
            whitened,
            pltpu.VMEM((channels * GROUP, 2 * BAND), jnp.bfloat16),
            pltpu.VMEM((steps, n_hour, channels * GROUP, quarter), jnp.bfloat16),
            pltpu.VMEM((steps, n_hour - 1, channels * GROUP, quarter), jnp.bfloat16),
            pltpu.VMEM((channels, NSHIFT, channels, quarter), jnp.float32),
            pltpu.SemaphoreType.DMA((chunks,)),
            pltpu.SemaphoreType.DMA((chunks,)),
            pltpu.SemaphoreType.DMA((chunks,)),
            pltpu.SemaphoreType.DMA((chunks,)),
            pltpu.SemaphoreType.DMA((steps, n_hour - 1)),
            pltpu.SemaphoreType.DMA((steps, n_hour - 1)),
        ],
        compiler_params=pltpu.CompilerParams(
            collective_id=0, has_side_effects=True, vmem_limit_bytes=48 * 1024 * 1024
        ),
        name="correlate",
    )(
        records.reshape(channels * windows, samples),
        live,
        jnp.asarray(forward_table()),
        jnp.asarray(inside.astype(ml_dtypes.bfloat16)),
        jnp.asarray(weight),
        jnp.asarray(inverse_table()),
    )


def solution(mesh):
    placed = (P("chan", "hour", None), P("chan"), P("hour"))
    return jax.shard_map(
        local, mesh=mesh, in_specs=placed, out_specs=P("chan", None, None, "hour"), check_vma=False
    )
```

profile of v0, /device:TPU:0, one launch (start us, length us, event | category | flops | bytes accessed | tf_op | source)
XLA Modules:
  0.0 75.1 jit_solution(17393514648205095293)
XLA Ops:
  0.0 0.7 convert_element_type.6
  0.7 0.7 convert_element_type.7
  1.3 0.1 broadcast_multiply_fusion
  1.4 0.2 mul.27.live
  1.6 0.0 copy-start
  1.6 1.7 %copy-done = bf16[40,16,2048]{2,1,0:T(8,128)(2,1)S(1)} copy-done((bf16[40,16,2048]{2,1,0:T(8,128)(2,1)S(1)}, bf16[40,16,2048]{2,1,0:T(8,128)(2,1)}, u32[]{:S(2)}) %copy-start) | copy-done | bytes 2621464
  3.3 0.0 copy-start.1
  3.3 1.2 %copy-done.1 = bf16[1024,512]{1,0:T(8,128)(2,1)S(1)} copy-done((bf16[1024,512]{1,0:T(8,128)(2,1)S(1)}, bf16[1024,512]{1,0:T(8,128)(2,1)}, u32[]{:S(2)}) %copy-start.1) | copy-done | bytes 1048600
  4.6 0.0 copy-start.2
  4.6 1.0 %copy-done.2 = bf16[512,512]{1,0:T(8,128)(2,1)S(1)} copy-done((bf16[512,512]{1,0:T(8,128)(2,1)S(1)}, bf16[512,512]{1,0:T(8,128)(2,1)}, u32[]{:S(2)}) %copy-start.2) | copy-done | bytes 524312
  5.6 0.0 copy-start.3
  5.6 0.7 copy-done.3
  6.3 68.0 %correlate.1 = bf16[40,2,40,128]{3,2,1,0:T(8,128)(2,1)S(1)} custom-call(bf16[640,2048]{1,0:T(8,128)(2,1)S(1)} %bitcast.1, f32[640,1]{1,0:T(8,128)S(1)} %mul.27.live, bf16[2048,1024]{1,0:T(8,128)(2,1)} %constant.8.clone.forward, bf16[512,512]{1,0:T(8,128)(2,1)S(1)} %copy-done.2, f32[1,512]{1,0:T(1,128)S(1)} %copy-done.3, bf16[1024,512]{1,0:T(8,128)(2,1)S(1)} %copy-done.1), custom_call_target="tpu_custom_call" | custom-call | tf_op jit(solution)/shard_map/correlate/pallas_call | solution.py:205
  74.2 0.9 %copy.10 = bf16[40,2,40,128]{3,2,1,0:T(8,128)(2,1)} copy(bf16[40,2,40,128]{3,2,1,0:T(8,128)(2,1)S(1)} %correlate.1) | data formatting | bytes 1638400
Async XLA Ops:
  1.6 1.7 %copy-start = (bf16[40,16,2048]{2,1,0:T(8,128)(2,1)S(1)}, bf16[40,16,2048]{2,1,0:T(8,128)(2,1)}, u32[]{:S(2)}) copy-start(bf16[40,16,2048]{2,1,0:T(8,128)(2,1)} %param.7) | copy-start | bytes 7864324
  3.3 1.2 %copy-start.1 = (bf16[1024,512]{1,0:T(8,128)(2,1)S(1)}, bf16[1024,512]{1,0:T(8,128)(2,1)}, u32[]{:S(2)}) copy-start(bf16[1024,512]{1,0:T(8,128)(2,1)} %constant.11.clone.inverse) | copy-start | bytes 3145732
  4.6 1.0 %copy-start.2 = (bf16[512,512]{1,0:T(8,128)(2,1)S(1)}, bf16[512,512]{1,0:T(8,128)(2,1)}, u32[]{:S(2)}) copy-start(bf16[512,512]{1,0:T(8,128)(2,1)} %constant.9.clone.inside) | copy-start | bytes 1572868
  5.6 0.7 copy-start.3
where the time goes:
time: 75.7 us; the launch traced here: 75.1 us
  Pallas kernels  68 us (90%)
  local copies, waits for them, and re-layouts  5.78 us (8%)
  other arithmetic  1.39 us (2%)
    pallas_call x1, Pallas kernels, local(): pl.pallas_call(functools.partial(kernel, n_chan, n_hour, channels, window...  68 us
    unnamed x9, local copies, waits for them, and re-layouts  5.58 us

commit v1 on v0

v1 whole, which is shorter than its diff:
```python
import functools
import math

import jax
import jax.numpy as jnp
import ml_dtypes
import numpy as np
from jax import lax
from jax.experimental import pallas as pl
from jax.experimental.pallas import tpu as pltpu
from jax.sharding import PartitionSpec as P

SAMPLES = 2048
BAND = 512
FIRST_BIN = 32
HALF = 64
LAGS = 512
NSHIFT = 2
GROUP = 8
LANES = 128
MESH = pl.DeviceIdType.MESH


def forward_table():
    times = np.arange(SAMPLES)[:, None]
    bins = FIRST_BIN + np.arange(BAND)[None, :]
    angle = (times * bins % SAMPLES) * (2.0 * math.pi / SAMPLES)
    return np.concatenate([np.cos(angle), -np.sin(angle)], axis=1).astype(ml_dtypes.bfloat16)


def inverse_table():
    bins = FIRST_BIN + np.arange(BAND)[:, None]
    shifts = np.arange(LAGS)[None, :] - LAGS // 2
    angle = (bins * shifts % SAMPLES) * (2.0 * math.pi / SAMPLES)
    return np.concatenate([np.cos(angle), -np.sin(angle)], axis=0).astype(ml_dtypes.bfloat16)


def band_inside():
    index = np.arange(BAND)
    return np.abs(index[:, None] - index[None, :]) <= HALF


def kernel(
    n_chan, n_hour, channels, windows, norm_factor,
    records_hbm, channels_hbm, windows_hbm, forward_hbm, inside_hbm, weight_hbm, inverse_hbm, out,
    records, live_channels, live_windows, forward, inside, weight, inverse,
    own, own_send, far_two, far_one, far, cross, lagged, heard, total,
    load_sem, record_sem, two_send, two_recv, one_send, one_recv, sum_send, sum_recv,
):
    chunks = channels // GROUP
    rows = GROUP * windows
    quarter = LAGS // n_hour
    tiles = BAND // LANES
    me = lax.axis_index("chan")
    hour = lax.axis_index("hour")
    parity = lax.rem(me, 2)
    before = lax.rem(me + n_chan - 2, n_chan)
    after = lax.rem(me + 2, n_chan)
    twin = me + 1 - 2 * parity

    record_loads = []
    for chunk in range(chunks):
        at = pl.ds(chunk * rows, rows)
        record_loads.append(
            pltpu.make_async_copy(records_hbm.at[at, :], records.at[at, :], record_sem.at[chunk])
        )
    pairs = (
        (forward_hbm, forward), (channels_hbm, live_channels), (windows_hbm, live_windows),
        (inside_hbm, inside), (weight_hbm, weight), (inverse_hbm, inverse),
    )
    loads = [pltpu.make_async_copy(*pair, load_sem.at[n]) for n, pair in enumerate(pairs)]
    record_loads[0].start()
    for load in loads:
        load.start()
    for load in record_loads[1:]:
        load.start()

    barrier = pltpu.get_barrier_semaphore()
    for chan in (before, after, twin):
        pl.semaphore_signal(barrier, inc=1, device_id=(chan, hour), device_id_type=MESH)
    for step in range(1, n_hour):
        other = lax.rem(hour + step, n_hour)
        pl.semaphore_signal(barrier, inc=1, device_id=(me, other), device_id_type=MESH)

    def to_before(chunk):
        return pltpu.make_async_remote_copy(
            src_ref=own_send.at[chunk], dst_ref=far_two.at[chunk],
            send_sem=two_send.at[chunk], recv_sem=two_recv.at[chunk],
            device_id=(before, hour), device_id_type=MESH,
        )

    def to_twin(source, chunk):
        return pltpu.make_async_remote_copy(
            src_ref=source.at[chunk], dst_ref=far_one.at[chunk],
            send_sem=one_send.at[chunk], recv_sem=one_recv.at[chunk],
            device_id=(twin, hour), device_id_type=MESH,
        )

    def to_hour(step, distance):
        target = lax.rem(hour + distance, n_hour)
        return pltpu.make_async_remote_copy(
            src_ref=lagged.at[step, target], dst_ref=heard.at[step, distance - 1],
            send_sem=sum_send.at[step, distance - 1], recv_sem=sum_recv.at[step, distance - 1],
            device_id=(me, target), device_id_type=MESH,
        )

    for load in loads:
        load.wait()
    pl.semaphore_wait(barrier, 3 + n_hour - 1)

    def whiten_chunk(chunk, carry):
        start = pl.multiple_of(chunk * rows, rows)
        at = pl.ds(start, rows)
        pltpu.make_async_copy(
            records_hbm.at[at, :], records.at[at, :], record_sem.at[chunk]
        ).wait()
        spectra = jnp.dot(records[at, :], forward[...], preferred_element_type=jnp.float32)
        real_part = spectra[:, :BAND]
        imag_part = spectra[:, BAND:]
        amplitude = jnp.sqrt(real_part * real_part + imag_part * imag_part)
        high = amplitude.astype(jnp.bfloat16)
        low = (amplitude - high.astype(jnp.float32)).astype(jnp.bfloat16)
        smooth = jnp.dot(high, inside[...], preferred_element_type=jnp.float32)
        smooth = smooth + jnp.dot(low, inside[...], preferred_element_type=jnp.float32)
        row = lax.broadcasted_iota(jnp.int32, (rows, channels), 0)
        lane = lax.broadcasted_iota(jnp.int32, (rows, channels), 1)
        picked = jnp.where(lane == chunk * GROUP + row // windows, live_channels[...], 0)
        live = jnp.sum(picked.astype(jnp.float32), axis=1, keepdims=True)
        row = lax.broadcasted_iota(jnp.int32, (rows, windows), 0)
        lane = lax.broadcasted_iota(jnp.int32, (rows, windows), 1)
        picked = jnp.where(lane == row % windows, live_windows[...], 0)
        live = live * jnp.sum(picked.astype(jnp.float32), axis=1, keepdims=True)
        factor = live / (smooth * weight[...] + 1e-06)
        for tile in range(tiles):
            lanes = slice(tile * LANES, (tile + 1) * LANES)
            real = (real_part[:, lanes] * factor[:, lanes]).astype(jnp.bfloat16).astype(jnp.float32)
            imag = (imag_part[:, lanes] * factor[:, lanes]).astype(jnp.bfloat16).astype(jnp.float32)
            for kind, value in enumerate((real, imag, real - imag, real + imag)):
                own[kind, tile, at, :] = value
        for kind in range(2):
            for tile in range(tiles):
                for pair in range(windows // 2):
                    both = [
                        own[kind, tile, pl.ds(start + 2 * pair + part, GROUP, stride=windows), :]
                        for part in range(2)
                    ]
                    own_send[
                        chunk, pl.ds(pair * 2 * GROUP, 2 * GROUP),
                        pl.ds(kind * BAND + tile * LANES, LANES),
                    ] = jnp.concatenate(both, axis=0).astype(jnp.bfloat16)
        to_before(chunk).start()

        @pl.when(parity == 1)
        def _():
            to_twin(own_send, chunk).start()

        return carry

    lax.fori_loop(0, chunks, whiten_chunk, 0)

    def cross_lags(blocks):
        batch = 4
        count = len(blocks)
        for place, (source, chunk, _) in enumerate(blocks):
            for tile in range(tiles):
                real = source[chunk, :, pl.ds(tile * LANES, LANES)].astype(jnp.float32)
                imag = source[chunk, :, pl.ds(BAND + tile * LANES, LANES)].astype(jnp.float32)
                far[place, 0, tile] = real + imag
                far[place, 1, tile] = imag
                far[place, 2, tile] = real

        def tile_step(tile, carry):
            def channel_step(index, inner):
                sums = [[[None] * 3 for _ in range(batch)] for _ in range(count)]
                for window in range(windows):
                    at = pl.ds(window * GROUP, GROUP)
                    far_here = [[far[p, kind, tile, at, :] for kind in range(3)] for p in range(count)]
                    for part in range(batch):
                        base = pl.multiple_of((batch * index + part) * windows, windows)
                        for kind, stored in enumerate((0, 2, 3)):
                            mine = own[stored, tile, pl.ds(base + window, GROUP, stride=0), :]
                            for p in range(count):
                                term = mine * far_here[p][kind]
                                old = sums[p][part][kind]
                                sums[p][part][kind] = term if old is None else old + term
                size = batch * GROUP
                at = pl.ds(pl.multiple_of(index * size, size), size)
                lanes = pl.multiple_of(tile * LANES, LANES)
                for p in range(count):
                    reals = [k[0] - k[1] for k in sums[p]]
                    imags = [k[0] - k[2] for k in sums[p]]
                    cross[p, at, pl.ds(lanes, LANES)] = jnp.concatenate(reals, axis=0).astype(
                        jnp.bfloat16
                    )
                    cross[p, at, pl.ds(BAND + lanes, LANES)] = jnp.concatenate(
                        imags, axis=0
                    ).astype(jnp.bfloat16)
                return inner

            return lax.fori_loop(0, channels // batch, channel_step, carry)

        lax.fori_loop(0, tiles, tile_step, 0)
        for p, (_, _, step) in enumerate(blocks):
            result = jnp.dot(cross[p], inverse[...], preferred_element_type=jnp.float32)
            result = result * norm_factor
            for part in range(n_hour):
                lanes = slice(part * quarter, (part + 1) * quarter)
                lagged[step, part] = result[:, lanes].astype(jnp.bfloat16)
            for distance in range(1, n_hour):
                to_hour(step, distance).start()

    def finish(chunk, shift):
        step = 2 * chunk + shift
        value = lagged[step, hour].astype(jnp.float32)
        for distance in range(1, n_hour):
            to_hour(step, distance).wait()
            value = value + heard[step, distance - 1].astype(jnp.float32)
        at = pl.ds(pl.multiple_of(chunk * GROUP, GROUP), GROUP)
        total[:, shift, at, :] = value.reshape(channels, GROUP, quarter)

    def take_two(chunk):
        to_before(chunk).wait_recv()

        @pl.when(parity == 0)
        def _():
            to_twin(far_two, chunk).start()

    take_two(0)
    cross_lags([(far_two, 0, 1)])

    def correlate_chunk(chunk, carry):
        take_two(chunk + 1)
        to_twin(own_send, chunk).wait_recv()
        cross_lags([(far_two, chunk + 1, 2 * chunk + 3), (far_one, chunk, 2 * chunk)])

        @pl.when(chunk >= 1)
        def _():
            finish(chunk - 1, 1)

        @pl.when(chunk >= 2)
        def _():
            finish(chunk - 2, 0)

        return carry

    lax.fori_loop(0, chunks - 1, correlate_chunk, 0)
    last = chunks - 1
    to_twin(own_send, last).wait_recv()
    cross_lags([(far_one, last, 2 * last)])
    for chunk in range(chunks):
        to_before(chunk).wait_send()
        to_twin(own_send, chunk).wait_send()
    for chunk in range(max(chunks - 2, 0), chunks):
        finish(chunk, 1)
    for chunk in range(max(chunks - 3, 0), chunks):
        finish(chunk, 0)
    out[...] = total[...].astype(jnp.bfloat16)


def local(records, live_channels, live_windows):
    channels, windows, samples = records.shape
    n_chan, n_hour = lax.axis_size("chan"), lax.axis_size("hour")
    norm_factor = 1.0 / math.sqrt(windows * n_hour * BAND)
    chunks, rows, quarter = channels // GROUP, GROUP * windows, LAGS // n_hour
    steps = NSHIFT * chunks
    inside = band_inside()
    weight = (1.0 / inside.sum(axis=0, keepdims=True)).astype(np.float32)
    whitened = pltpu.VMEM((chunks, rows, 2 * BAND), jnp.bfloat16)
    return pl.pallas_call(
        functools.partial(kernel, n_chan, n_hour, channels, windows, norm_factor),
        out_shape=jax.ShapeDtypeStruct((channels, NSHIFT, channels, quarter), jnp.bfloat16),
        in_specs=[pl.BlockSpec(memory_space=pltpu.HBM)] * 7,
        out_specs=pl.BlockSpec(memory_space=pltpu.VMEM),
        scratch_shapes=[
            pltpu.VMEM((channels * windows, samples), jnp.bfloat16),
            pltpu.VMEM((1, channels), jnp.int32),
            pltpu.VMEM((1, windows), jnp.int32),
            pltpu.VMEM((SAMPLES, 2 * BAND), jnp.bfloat16),
            pltpu.VMEM((BAND, BAND), jnp.bfloat16),
            pltpu.VMEM((1, BAND), jnp.float32),
            pltpu.VMEM((2 * BAND, LAGS), jnp.bfloat16),
            pltpu.VMEM((4, BAND // LANES, channels * windows, LANES), jnp.float32),
            whitened,
            whitened,
            whitened,
            pltpu.VMEM((NSHIFT, 3, BAND // LANES, rows, LANES), jnp.float32),
            pltpu.VMEM((NSHIFT, channels * GROUP, 2 * BAND), jnp.bfloat16),
            pltpu.VMEM((steps, n_hour, channels * GROUP, quarter), jnp.bfloat16),
            pltpu.VMEM((steps, n_hour - 1, channels * GROUP, quarter), jnp.bfloat16),
            pltpu.VMEM((channels, NSHIFT, channels, quarter), jnp.float32),
            pltpu.SemaphoreType.DMA((6,)),
            pltpu.SemaphoreType.DMA((chunks,)),
            pltpu.SemaphoreType.DMA((chunks,)),
            pltpu.SemaphoreType.DMA((chunks,)),
            pltpu.SemaphoreType.DMA((chunks,)),
            pltpu.SemaphoreType.DMA((chunks,)),
            pltpu.SemaphoreType.DMA((steps, n_hour - 1)),
            pltpu.SemaphoreType.DMA((steps, n_hour - 1)),
        ],
        compiler_params=pltpu.CompilerParams(
            collective_id=0, has_side_effects=True, vmem_limit_bytes=64 * 1024 * 1024
        ),
        name="correlate",
    )(
        records.reshape(channels * windows, samples),
        live_channels.reshape(1, channels),
        live_windows.reshape(1, windows),
        jnp.asarray(forward_table()),
        jnp.asarray(inside.astype(ml_dtypes.bfloat16)),
        jnp.asarray(weight),
        jnp.asarray(inverse_table()),
    )


def solution(mesh):
    placed = (P("chan", "hour", None), P("chan"), P("hour"))
    return jax.shard_map(
        local, mesh=mesh, in_specs=placed, out_specs=P("chan", None, None, "hour"), check_vma=False
    )
```

time: 75.7 us -> 61.6 us (0.81)
  Pallas kernels: 68 us -> 59.1 us
  local copies, waits for them, and re-layouts: 5.78 us -> 2.11 us
  other arithmetic: 1.39 us -> 0 us
    pallas_call x1, Pallas kernels: 68 us -> 59.1 us  [local(): pl.pallas_call(functools.partial(kernel, n_chan, n_hour, channels, window...]
    unnamed x9 -> x1, local copies, waits for them, and re-layouts: 5.58 us -> 2.11 us
    convert_element_type x2 -> x0, other arithmetic: 1.31 us -> none  [the longest x1 0.66 us: local(): live_channels.astype(jnp.float32)[:, None]]
where the time goes in v1:
time: 61.6 us; the launch traced here: 61.2 us
  Pallas kernels  59.1 us (96%)
  local copies, waits for them, and re-layouts  2.11 us (3%)
    pallas_call x1, Pallas kernels, local(): pl.pallas_call(functools.partial(kernel, n_chan, n_hour, channels, window...  59.1 us
    unnamed x1, local copies, waits for them, and re-layouts  2.11 us

profile of v1, /device:TPU:0, one launch (start us, length us, event | category | flops | bytes accessed | tf_op | source)
XLA Modules:
  0.0 61.2 jit_solution(8070791973860104826)
XLA Ops:
  0.0 59.1 %correlate.1 = bf16[40,2,40,128]{3,2,1,0:T(8,128)(2,1)} custom-call(bf16[640,2048]{1,0:T(8,128)(2,1)} %bitcast.3, s32[1,40]{1,0:T(1,128)} %bitcast.4, s32[1,16]{1,0:T(1,128)} %bitcast.5, bf16[2048,1024]{1,0:T(8,128)(2,1)} %constant.8.clone.forward_hbm, bf16[512,512]{1,0:T(8,128)(2,1)} %constant.9.clone.inside_hbm, f32[1,512]{1,0:T(1,128)} %constant.10.clone.weight_hbm, ...), custom_call_target="tpu_custom_call" | custom-call | tf_op jit(solution)/shard_map/correlate/pallas_call | solution.py:269
  59.1 2.1 %copy.9 = bf16[40,2,40,128]{3,2,1,0:T(8,128)(2,1)} copy(bf16[40,2,40,128]{3,2,1,0:T(8,128)(2,1)} %correlate.1) | data formatting | bytes 1638400

commit v2 on v1

--- a/solution.py
+++ b/solution.py
@@ -42,9 +42,9 @@
 
 def kernel(
     n_chan, n_hour, channels, windows, norm_factor,
-    records_hbm, channels_hbm, windows_hbm, forward_hbm, inside_hbm, weight_hbm, inverse_hbm, out,
+    records_hbm, channels_hbm, windows_hbm, forward_hbm, inside_hbm, weight_hbm, inverse_hbm, total,
     records, live_channels, live_windows, forward, inside, weight, inverse,
-    own, own_send, far_two, far_one, far, cross, lagged, heard, total,
+    spectra, own, own_send, far_two, far_one, far, cross, lagged, heard,
     load_sem, record_sem, two_send, two_recv, one_send, one_recv, sum_send, sum_recv,
 ):
     chunks = channels // GROUP
@@ -111,17 +111,15 @@
     def whiten_chunk(chunk, carry):
         start = pl.multiple_of(chunk * rows, rows)
         at = pl.ds(start, rows)
-        pltpu.make_async_copy(
-            records_hbm.at[at, :], records.at[at, :], record_sem.at[chunk]
-        ).wait()
-        spectra = jnp.dot(records[at, :], forward[...], preferred_element_type=jnp.float32)
-        real_part = spectra[:, :BAND]
-        imag_part = spectra[:, BAND:]
+        real_part = spectra[at, :BAND]
+        imag_part = spectra[at, BAND:]
         amplitude = jnp.sqrt(real_part * real_part + imag_part * imag_part)
         high = amplitude.astype(jnp.bfloat16)
         low = (amplitude - high.astype(jnp.float32)).astype(jnp.bfloat16)
-        smooth = jnp.dot(high, inside[...], preferred_element_type=jnp.float32)
-        smooth = smooth + jnp.dot(low, inside[...], preferred_element_type=jnp.float32)
+        smooth = jnp.dot(
+            jnp.concatenate([high, low], axis=0), inside[...], preferred_element_type=jnp.float32
+        )
+        smooth = smooth[:rows] + smooth[rows:]
         row = lax.broadcasted_iota(jnp.int32, (rows, channels), 0)
         lane = lax.broadcasted_iota(jnp.int32, (rows, channels), 1)
         picked = jnp.where(lane == chunk * GROUP + row // windows, live_channels[...], 0)
@@ -156,11 +154,20 @@
 
         return carry
 
-    lax.fori_loop(0, chunks, whiten_chunk, 0)
+    def transform(first, count):
+        at = pl.ds(first * rows, count * rows)
+        for load in record_loads[first : first + count]:
+            load.wait()
+        spectra[at, :] = jnp.dot(records[at, :], forward[...], preferred_element_type=jnp.float32)
+
+    transform(0, 1)
+    whiten_chunk(0, 0)
+    transform(1, chunks - 1)
+    lax.fori_loop(1, chunks, whiten_chunk, 0)
 
     def cross_lags(blocks):
-        batch = 4
         count = len(blocks)
+        batch = 8 // count
         for place, (source, chunk, _) in enumerate(blocks):
             for tile in range(tiles):
                 real = source[chunk, :, pl.ds(tile * LANES, LANES)].astype(jnp.float32)
@@ -254,7 +261,6 @@
         finish(chunk, 1)
     for chunk in range(max(chunks - 3, 0), chunks):
         finish(chunk, 0)
-    out[...] = total[...].astype(jnp.bfloat16)
 
 
 def local(records, live_channels, live_windows):
@@ -268,7 +274,7 @@
     whitened = pltpu.VMEM((chunks, rows, 2 * BAND), jnp.bfloat16)
     return pl.pallas_call(
         functools.partial(kernel, n_chan, n_hour, channels, windows, norm_factor),
-        out_shape=jax.ShapeDtypeStruct((channels, NSHIFT, channels, quarter), jnp.bfloat16),
+        out_shape=jax.ShapeDtypeStruct((channels, NSHIFT, channels, quarter), jnp.float32),
         in_specs=[pl.BlockSpec(memory_space=pltpu.HBM)] * 7,
         out_specs=pl.BlockSpec(memory_space=pltpu.VMEM),
         scratch_shapes=[
@@ -279,6 +285,7 @@
             pltpu.VMEM((BAND, BAND), jnp.bfloat16),
             pltpu.VMEM((1, BAND), jnp.float32),
             pltpu.VMEM((2 * BAND, LAGS), jnp.bfloat16),
+            pltpu.VMEM((channels * windows, 2 * BAND), jnp.float32),
             pltpu.VMEM((4, BAND // LANES, channels * windows, LANES), jnp.float32),
             whitened,
             whitened,
@@ -287,7 +294,6 @@
             pltpu.VMEM((NSHIFT, channels * GROUP, 2 * BAND), jnp.bfloat16),
             pltpu.VMEM((steps, n_hour, channels * GROUP, quarter), jnp.bfloat16),
             pltpu.VMEM((steps, n_hour - 1, channels * GROUP, quarter), jnp.bfloat16),
-            pltpu.VMEM((channels, NSHIFT, channels, quarter), jnp.float32),
             pltpu.SemaphoreType.DMA((6,)),
             pltpu.SemaphoreType.DMA((chunks,)),
             pltpu.SemaphoreType.DMA((chunks,)),
@@ -309,7 +315,7 @@
         jnp.asarray(inside.astype(ml_dtypes.bfloat16)),
         jnp.asarray(weight),
         jnp.asarray(inverse_table()),
-    )
+    ).astype(jnp.bfloat16)
 
 
 def solution(mesh):

time: 61.6 us -> 62.1 us (level)
  other arithmetic: 0 us -> 2.43 us
  local copies, waits for them, and re-layouts: 2.11 us -> 0 us
    convert_element_type x0 -> x1, other arithmetic: none -> 2.43 us  [local(): return pl.pallas_call(functools.partial(kernel, n_chan, n_hour, channels,...]
    unnamed x1 -> x0, local copies, waits for them, and re-layouts: 2.11 us -> none
where the time goes in v2:
time: 62.1 us; the launch traced here: 61.8 us
  Pallas kernels  59.3 us (95%)
  other arithmetic  2.43 us (4%)
    pallas_call x1, Pallas kernels, local(): pl.pallas_call(functools.partial(kernel, n_chan, n_hour, channels, window...  59.3 us
    convert_element_type x1, other arithmetic, local(): return pl.pallas_call(functools.partial(kernel, n_chan, n_hour, channels,...  2.43 us

profile of v2, /device:TPU:0, one launch (start us, length us, event | category | flops | bytes accessed | tf_op | source)
XLA Modules:
  0.0 61.8 jit_solution(292429844087481032)
XLA Ops:
  0.0 59.3 %correlate.1 = f32[40,2,40,128]{3,2,1,0:T(8,128)} custom-call(bf16[640,2048]{1,0:T(8,128)(2,1)} %bitcast.3, s32[1,40]{1,0:T(1,128)} %bitcast.4, s32[1,16]{1,0:T(1,128)} %bitcast.5, bf16[2048,1024]{1,0:T(8,128)(2,1)} %constant.8.clone.forward_hbm, bf16[512,512]{1,0:T(8,128)(2,1)} %constant.9.clone.inside_hbm, f32[1,512]{1,0:T(1,128)} %constant.10.clone.weight_hbm, ...), custom_call_target="tpu_custom_call" | custom-call | tf_op jit(solution)/shard_map/correlate/pallas_call | solution.py:275
  59.3 2.4 %convert_element_type.3 = bf16[40,2,40,128]{3,2,1,0:T(8,128)(2,1)} convert(f32[40,2,40,128]{3,2,1,0:T(8,128)} %correlate.1) | non-fusion elementwise | flops 409600 | bytes 2457600 | tf_op jit(solution)/shard_map/convert_element_type | solution.py:318

commit v3 on v2

--- a/solution.py
+++ b/solution.py
@@ -42,10 +42,10 @@
 
 def kernel(
     n_chan, n_hour, channels, windows, norm_factor,
-    records_hbm, channels_hbm, windows_hbm, forward_hbm, inside_hbm, weight_hbm, inverse_hbm, total,
+    records_hbm, channels_hbm, windows_hbm, forward_hbm, inside_hbm, weight_hbm, inverse_hbm, out,
     records, live_channels, live_windows, forward, inside, weight, inverse,
-    spectra, own, own_send, far_two, far_one, far, cross, lagged, heard,
-    load_sem, record_sem, two_send, two_recv, one_send, one_recv, sum_send, sum_recv,
+    spectra, own, own_send, far_two, far_one, far, cross, lagged, near, joined, heard, total,
+    load_sem, record_sem, two_send, two_recv, one_send, one_recv, near_send, near_recv, sum_send, sum_recv,
 ):
     chunks = channels // GROUP
     rows = GROUP * windows
@@ -57,6 +57,10 @@
     before = lax.rem(me + n_chan - 2, n_chan)
     after = lax.rem(me + 2, n_chan)
     twin = me + 1 - 2 * parity
+    core = lax.rem(hour, 2)
+    chip = hour // 2
+    other_core = hour + 1 - 2 * core
+    other_chip = lax.rem(hour + 2, 4)
 
     record_loads = []
     for chunk in range(chunks):
@@ -78,8 +82,7 @@
     barrier = pltpu.get_barrier_semaphore()
     for chan in (before, after, twin):
         pl.semaphore_signal(barrier, inc=1, device_id=(chan, hour), device_id_type=MESH)
-    for step in range(1, n_hour):
-        other = lax.rem(hour + step, n_hour)
+    for other in (other_core, other_chip):
         pl.semaphore_signal(barrier, inc=1, device_id=(me, other), device_id_type=MESH)
 
     def to_before(chunk):
@@ -96,17 +99,23 @@
             device_id=(twin, hour), device_id_type=MESH,
         )
 
-    def to_hour(step, distance):
-        target = lax.rem(hour + distance, n_hour)
+    def to_core(step):
         return pltpu.make_async_remote_copy(
-            src_ref=lagged.at[step, target], dst_ref=heard.at[step, distance - 1],
-            send_sem=sum_send.at[step, distance - 1], recv_sem=sum_recv.at[step, distance - 1],
-            device_id=(me, target), device_id_type=MESH,
+            src_ref=lagged.at[step, 1 - core], dst_ref=near.at[step],
+            send_sem=near_send.at[step], recv_sem=near_recv.at[step],
+            device_id=(me, other_core), device_id_type=MESH,
+        )
+
+    def to_chip(step):
+        return pltpu.make_async_remote_copy(
+            src_ref=joined.at[step], dst_ref=heard.at[step],
+            send_sem=sum_send.at[step], recv_sem=sum_recv.at[step],
+            device_id=(me, other_chip), device_id_type=MESH,
         )
 
     for load in loads:
         load.wait()
-    pl.semaphore_wait(barrier, 3 + n_hour - 1)
+    pl.semaphore_wait(barrier, 5)
 
     def whiten_chunk(chunk, carry):
         start = pl.multiple_of(chunk * rows, rows)
@@ -165,7 +174,7 @@
     transform(1, chunks - 1)
     lax.fori_loop(1, chunks, whiten_chunk, 0)
 
-    def cross_lags(blocks):
+    def cross_lags(blocks, between):
         count = len(blocks)
         batch = 8 // count
         for place, (source, chunk, _) in enumerate(blocks):
@@ -204,6 +213,7 @@
                     ).astype(jnp.bfloat16)
                 return inner
 
+            pl.when(tile == 1)(between)
             return lax.fori_loop(0, channels // batch, channel_step, carry)
 
         lax.fori_loop(0, tiles, tile_step, 0)
@@ -212,16 +222,22 @@
             result = result * norm_factor
             for part in range(n_hour):
                 lanes = slice(part * quarter, (part + 1) * quarter)
-                lagged[step, part] = result[:, lanes].astype(jnp.bfloat16)
-            for distance in range(1, n_hour):
-                to_hour(step, distance).start()
+                lagged[step, part % 2, part // 2] = result[:, lanes].astype(jnp.bfloat16)
+            to_core(step).start()
+
+    def relay(step):
+        to_core(step).wait_recv()
+        mine = lagged[step, core, 1 - chip].astype(jnp.float32)
+        mine = mine + near[step, 1 - chip].astype(jnp.float32)
+        joined[step] = mine.astype(jnp.bfloat16)
+        to_chip(step).start()
 
     def finish(chunk, shift):
         step = 2 * chunk + shift
-        value = lagged[step, hour].astype(jnp.float32)
-        for distance in range(1, n_hour):
-            to_hour(step, distance).wait()
-            value = value + heard[step, distance - 1].astype(jnp.float32)
+        to_core(step).wait_send()
+        to_chip(step).wait()
+        value = lagged[step, core, chip].astype(jnp.float32)
+        value = value + near[step, chip].astype(jnp.float32) + heard[step].astype(jnp.float32)
         at = pl.ds(pl.multiple_of(chunk * GROUP, GROUP), GROUP)
         total[:, shift, at, :] = value.reshape(channels, GROUP, quarter)
 
@@ -233,12 +249,19 @@
             to_twin(far_two, chunk).start()
 
     take_two(0)
-    cross_lags([(far_two, 0, 1)])
+    cross_lags([(far_two, 0, 1)], lambda: None)
 
     def correlate_chunk(chunk, carry):
         take_two(chunk + 1)
         to_twin(own_send, chunk).wait_recv()
-        cross_lags([(far_two, chunk + 1, 2 * chunk + 3), (far_one, chunk, 2 * chunk)])
+        def between():
+            relay(2 * chunk + 1)
+
+            @pl.when(chunk >= 1)
+            def _():
+                relay(2 * chunk - 2)
+
+        cross_lags([(far_two, chunk + 1, 2 * chunk + 3), (far_one, chunk, 2 * chunk)], between)
 
         @pl.when(chunk >= 1)
         def _():
@@ -253,7 +276,13 @@
     lax.fori_loop(0, chunks - 1, correlate_chunk, 0)
     last = chunks - 1
     to_twin(own_send, last).wait_recv()
-    cross_lags([(far_one, last, 2 * last)])
+
+    def between_last():
+        relay(2 * last + 1)
+        relay(2 * last - 2)
+
+    cross_lags([(far_one, last, 2 * last)], between_last)
+    relay(2 * last)
     for chunk in range(chunks):
         to_before(chunk).wait_send()
         to_twin(own_send, chunk).wait_send()
@@ -261,6 +290,7 @@
         finish(chunk, 1)
     for chunk in range(max(chunks - 3, 0), chunks):
         finish(chunk, 0)
+    out[...] = total[...].astype(jnp.bfloat16)
 
 
 def local(records, live_channels, live_windows):
@@ -274,7 +304,7 @@
     whitened = pltpu.VMEM((chunks, rows, 2 * BAND), jnp.bfloat16)
     return pl.pallas_call(
         functools.partial(kernel, n_chan, n_hour, channels, windows, norm_factor),
-        out_shape=jax.ShapeDtypeStruct((channels, NSHIFT, channels, quarter), jnp.float32),
+        out_shape=jax.ShapeDtypeStruct((channels, NSHIFT, channels, quarter), jnp.bfloat16),
         in_specs=[pl.BlockSpec(memory_space=pltpu.HBM)] * 7,
         out_specs=pl.BlockSpec(memory_space=pltpu.VMEM),
         scratch_shapes=[
@@ -292,16 +322,21 @@
             whitened,
             pltpu.VMEM((NSHIFT, 3, BAND // LANES, rows, LANES), jnp.float32),
             pltpu.VMEM((NSHIFT, channels * GROUP, 2 * BAND), jnp.bfloat16),
-            pltpu.VMEM((steps, n_hour, channels * GROUP, quarter), jnp.bfloat16),
-            pltpu.VMEM((steps, n_hour - 1, channels * GROUP, quarter), jnp.bfloat16),
+            pltpu.VMEM((steps, 2, n_hour // 2, channels * GROUP, quarter), jnp.bfloat16),
+            pltpu.VMEM((steps, n_hour // 2, channels * GROUP, quarter), jnp.bfloat16),
+            pltpu.VMEM((steps, channels * GROUP, quarter), jnp.bfloat16),
+            pltpu.VMEM((steps, channels * GROUP, quarter), jnp.bfloat16),
+            pltpu.VMEM((channels, NSHIFT, channels, quarter), jnp.float32),
             pltpu.SemaphoreType.DMA((6,)),
             pltpu.SemaphoreType.DMA((chunks,)),
             pltpu.SemaphoreType.DMA((chunks,)),
             pltpu.SemaphoreType.DMA((chunks,)),
             pltpu.SemaphoreType.DMA((chunks,)),
             pltpu.SemaphoreType.DMA((chunks,)),
-            pltpu.SemaphoreType.DMA((steps, n_hour - 1)),
-            pltpu.SemaphoreType.DMA((steps, n_hour - 1)),
+            pltpu.SemaphoreType.DMA((steps,)),
+            pltpu.SemaphoreType.DMA((steps,)),
+            pltpu.SemaphoreType.DMA((steps,)),
+            pltpu.SemaphoreType.DMA((steps,)),
         ],
         compiler_params=pltpu.CompilerParams(
             collective_id=0, has_side_effects=True, vmem_limit_bytes=64 * 1024 * 1024
@@ -315,7 +350,7 @@
         jnp.asarray(inside.astype(ml_dtypes.bfloat16)),
         jnp.asarray(weight),
         jnp.asarray(inverse_table()),
-    ).astype(jnp.bfloat16)
+    )
 
 
 def solution(mesh):

time: 62.1 us -> 57 us (0.918)
  Pallas kernels: 59.3 us -> 54.8 us
  other arithmetic: 2.43 us -> 0 us
  local copies, waits for them, and re-layouts: 0 us -> 2.11 us
    pallas_call x1, Pallas kernels: 59.3 us -> 54.8 us  [local(): pl.pallas_call(functools.partial(kernel, n_chan, n_hour, channels, window...]
    convert_element_type x1 -> x0, other arithmetic: 2.43 us -> none  [local(): return pl.pallas_call(functools.partial(kernel, n_chan, n_hour, channels,...]
    unnamed x0 -> x1, local copies, waits for them, and re-layouts: none -> 2.11 us
where the time goes in v3:
time: 57 us; the launch traced here: 56.9 us
  Pallas kernels  54.8 us (96%)
  local copies, waits for them, and re-layouts  2.11 us (4%)
    pallas_call x1, Pallas kernels, local(): pl.pallas_call(functools.partial(kernel, n_chan, n_hour, channels, window...  54.8 us
    unnamed x1, local copies, waits for them, and re-layouts  2.11 us

profile of v3, /device:TPU:0, one launch (start us, length us, event | category | flops | bytes accessed | tf_op | source)
XLA Modules:
  0.0 56.9 jit_solution(18215668078021678136)
XLA Ops:
  0.0 54.8 %correlate.1 = bf16[40,2,40,128]{3,2,1,0:T(8,128)(2,1)} custom-call(bf16[640,2048]{1,0:T(8,128)(2,1)} %bitcast.3, s32[1,40]{1,0:T(1,128)} %bitcast.4, s32[1,16]{1,0:T(1,128)} %bitcast.5, bf16[2048,1024]{1,0:T(8,128)(2,1)} %constant.8.clone.forward_hbm, bf16[512,512]{1,0:T(8,128)(2,1)} %constant.9.clone.inside_hbm, f32[1,512]{1,0:T(1,128)} %constant.10.clone.weight_hbm, ...), custom_call_target="tpu_custom_call" | custom-call | tf_op jit(solution)/shard_map/correlate/pallas_call | solution.py:305
  54.8 2.1 %copy.9 = bf16[40,2,40,128]{3,2,1,0:T(8,128)(2,1)} copy(bf16[40,2,40,128]{3,2,1,0:T(8,128)(2,1)} %correlate.1) | data formatting | bytes 1638400

commit v4 on v3

--- a/solution.py
+++ b/solution.py
@@ -85,17 +85,17 @@
     for other in (other_core, other_chip):
         pl.semaphore_signal(barrier, inc=1, device_id=(me, other), device_id_type=MESH)
 
-    def to_before(chunk):
+    def to_before(chunk, tile):
         return pltpu.make_async_remote_copy(
-            src_ref=own_send.at[chunk], dst_ref=far_two.at[chunk],
-            send_sem=two_send.at[chunk], recv_sem=two_recv.at[chunk],
+            src_ref=own_send.at[chunk, tile], dst_ref=far_two.at[chunk, tile],
+            send_sem=two_send.at[chunk, tile], recv_sem=two_recv.at[chunk, tile],
             device_id=(before, hour), device_id_type=MESH,
         )
 
-    def to_twin(source, chunk):
+    def to_twin(source, chunk, tile):
         return pltpu.make_async_remote_copy(
-            src_ref=source.at[chunk], dst_ref=far_one.at[chunk],
-            send_sem=one_send.at[chunk], recv_sem=one_recv.at[chunk],
+            src_ref=source.at[chunk, tile], dst_ref=far_one.at[chunk, tile],
+            send_sem=one_send.at[chunk, tile], recv_sem=one_recv.at[chunk, tile],
             device_id=(twin, hour), device_id_type=MESH,
         )
 
@@ -144,22 +144,21 @@
             imag = (imag_part[:, lanes] * factor[:, lanes]).astype(jnp.bfloat16).astype(jnp.float32)
             for kind, value in enumerate((real, imag, real - imag, real + imag)):
                 own[kind, tile, at, :] = value
-        for kind in range(2):
-            for tile in range(tiles):
+        for tile in range(tiles):
+            for kind in range(2):
                 for pair in range(windows // 2):
                     both = [
                         own[kind, tile, pl.ds(start + 2 * pair + part, GROUP, stride=windows), :]
                         for part in range(2)
                     ]
                     own_send[
-                        chunk, pl.ds(pair * 2 * GROUP, 2 * GROUP),
-                        pl.ds(kind * BAND + tile * LANES, LANES),
+                        chunk, tile, pl.ds(pair * 2 * GROUP, 2 * GROUP), pl.ds(kind * LANES, LANES)
                     ] = jnp.concatenate(both, axis=0).astype(jnp.bfloat16)
-        to_before(chunk).start()
-
-        @pl.when(parity == 1)
-        def _():
-            to_twin(own_send, chunk).start()
+            to_before(chunk, tile).start()
+
+            @pl.when(parity == 1)
+            def _():
+                to_twin(own_send, chunk, tile).start()
 
         return carry
 
@@ -177,20 +176,29 @@
     def cross_lags(blocks, between):
         count = len(blocks)
         batch = 8 // count
-        for place, (source, chunk, _) in enumerate(blocks):
-            for tile in range(tiles):
-                real = source[chunk, :, pl.ds(tile * LANES, LANES)].astype(jnp.float32)
-                imag = source[chunk, :, pl.ds(BAND + tile * LANES, LANES)].astype(jnp.float32)
-                far[place, 0, tile] = real + imag
-                far[place, 1, tile] = imag
-                far[place, 2, tile] = real
-
         def tile_step(tile, carry):
+            for place, (source, chunk, _) in enumerate(blocks):
+                if source is far_two:
+                    to_before(chunk, tile).wait_recv()
+
+                    @pl.when(parity == 0)
+                    def _():
+                        to_twin(far_two, chunk, tile).start()
+
+                else:
+                    to_twin(own_send, chunk, tile).wait_recv()
+            for place, (source, chunk, _) in enumerate(blocks):
+                real = source[chunk, tile, :, :LANES].astype(jnp.float32)
+                imag = source[chunk, tile, :, LANES:].astype(jnp.float32)
+                far[place, 0] = real + imag
+                far[place, 1] = imag
+                far[place, 2] = real
+
             def channel_step(index, inner):
                 sums = [[[None] * 3 for _ in range(batch)] for _ in range(count)]
                 for window in range(windows):
                     at = pl.ds(window * GROUP, GROUP)
-                    far_here = [[far[p, kind, tile, at, :] for kind in range(3)] for p in range(count)]
+                    far_here = [[far[p, kind, at, :] for kind in range(3)] for p in range(count)]
                     for part in range(batch):
                         base = pl.multiple_of((batch * index + part) * windows, windows)
                         for kind, stored in enumerate((0, 2, 3)):
@@ -241,19 +249,9 @@
         at = pl.ds(pl.multiple_of(chunk * GROUP, GROUP), GROUP)
         total[:, shift, at, :] = value.reshape(channels, GROUP, quarter)
 
-    def take_two(chunk):
-        to_before(chunk).wait_recv()
-
-        @pl.when(parity == 0)
-        def _():
-            to_twin(far_two, chunk).start()
-
-    take_two(0)
     cross_lags([(far_two, 0, 1)], lambda: None)
 
     def correlate_chunk(chunk, carry):
-        take_two(chunk + 1)
-        to_twin(own_send, chunk).wait_recv()
         def between():
             relay(2 * chunk + 1)
 
@@ -275,7 +273,6 @@
 
     lax.fori_loop(0, chunks - 1, correlate_chunk, 0)
     last = chunks - 1
-    to_twin(own_send, last).wait_recv()
 
     def between_last():
         relay(2 * last + 1)
@@ -284,8 +281,9 @@
     cross_lags([(far_one, last, 2 * last)], between_last)
     relay(2 * last)
     for chunk in range(chunks):
-        to_before(chunk).wait_send()
-        to_twin(own_send, chunk).wait_send()
+        for tile in range(tiles):
+            to_before(chunk, tile).wait_send()
+            to_twin(own_send, chunk, tile).wait_send()
     for chunk in range(max(chunks - 2, 0), chunks):
         finish(chunk, 1)
     for chunk in range(max(chunks - 3, 0), chunks):
@@ -301,7 +299,8 @@
     steps = NSHIFT * chunks
     inside = band_inside()
     weight = (1.0 / inside.sum(axis=0, keepdims=True)).astype(np.float32)
-    whitened = pltpu.VMEM((chunks, rows, 2 * BAND), jnp.bfloat16)
+    tiles = BAND // LANES
+    whitened = pltpu.VMEM((chunks, tiles, rows, 2 * LANES), jnp.bfloat16)
     return pl.pallas_call(
         functools.partial(kernel, n_chan, n_hour, channels, windows, norm_factor),
         out_shape=jax.ShapeDtypeStruct((channels, NSHIFT, channels, quarter), jnp.bfloat16),
@@ -320,7 +319,7 @@
             whitened,
             whitened,
             whitened,
-            pltpu.VMEM((NSHIFT, 3, BAND // LANES, rows, LANES), jnp.float32),
+            pltpu.VMEM((NSHIFT, 3, rows, LANES), jnp.float32),
             pltpu.VMEM((NSHIFT, channels * GROUP, 2 * BAND), jnp.bfloat16),
             pltpu.VMEM((steps, 2, n_hour // 2, channels * GROUP, quarter), jnp.bfloat16),
             pltpu.VMEM((steps, n_hour // 2, channels * GROUP, quarter), jnp.bfloat16),
@@ -329,10 +328,10 @@
             pltpu.VMEM((channels, NSHIFT, channels, quarter), jnp.float32),
             pltpu.SemaphoreType.DMA((6,)),
             pltpu.SemaphoreType.DMA((chunks,)),
-            pltpu.SemaphoreType.DMA((chunks,)),
-            pltpu.SemaphoreType.DMA((chunks,)),
-            pltpu.SemaphoreType.DMA((chunks,)),
-            pltpu.SemaphoreType.DMA((chunks,)),
+            pltpu.SemaphoreType.DMA((chunks, tiles)),
+            pltpu.SemaphoreType.DMA((chunks, tiles)),
+            pltpu.SemaphoreType.DMA((chunks, tiles)),
+            pltpu.SemaphoreType.DMA((chunks, tiles)),
             pltpu.SemaphoreType.DMA((steps,)),
             pltpu.SemaphoreType.DMA((steps,)),
             pltpu.SemaphoreType.DMA((steps,)),

time: 57 us -> 55.1 us (0.967)
  Pallas kernels: 54.8 us -> 52.8 us
    pallas_call x1, Pallas kernels: 54.8 us -> 52.8 us  [local(): pl.pallas_call(functools.partial(kernel, n_chan, n_hour, channels, window...]
where the time goes in v4:
time: 55.1 us; the launch traced here: 55 us
  Pallas kernels  52.8 us (96%)
  local copies, waits for them, and re-layouts  2.11 us (4%)
    pallas_call x1, Pallas kernels, local(): pl.pallas_call(functools.partial(kernel, n_chan, n_hour, channels, window...  52.8 us
    unnamed x1, local copies, waits for them, and re-layouts  2.11 us

profile of v4, /device:TPU:0, one launch (start us, length us, event | category | flops | bytes accessed | tf_op | source)
XLA Modules:
  0.0 55.0 jit_solution(17724515516228644311)
XLA Ops:
  0.0 52.8 %correlate.1 = bf16[40,2,40,128]{3,2,1,0:T(8,128)(2,1)} custom-call(bf16[640,2048]{1,0:T(8,128)(2,1)} %bitcast.3, s32[1,40]{1,0:T(1,128)} %bitcast.4, s32[1,16]{1,0:T(1,128)} %bitcast.5, bf16[2048,1024]{1,0:T(8,128)(2,1)} %constant.8.clone.forward_hbm, bf16[512,512]{1,0:T(8,128)(2,1)} %constant.9.clone.inside_hbm, f32[1,512]{1,0:T(1,128)} %constant.10.clone.weight_hbm, ...), custom_call_target="tpu_custom_call" | custom-call | tf_op jit(solution)/shard_map/correlate/pallas_call | solution.py:304
  52.8 2.1 %copy.9 = bf16[40,2,40,128]{3,2,1,0:T(8,128)(2,1)} copy(bf16[40,2,40,128]{3,2,1,0:T(8,128)(2,1)} %correlate.1) | data formatting | bytes 1638400

commit v5 on v4

--- a/solution.py
+++ b/solution.py
@@ -74,9 +74,7 @@
     )
     loads = [pltpu.make_async_copy(*pair, load_sem.at[n]) for n, pair in enumerate(pairs)]
     record_loads[0].start()
-    for load in loads:
-        load.start()
-    for load in record_loads[1:]:
+    for load in loads[:-1]:
         load.start()
 
     barrier = pltpu.get_barrier_semaphore()
@@ -113,8 +111,10 @@
             device_id=(me, other_chip), device_id_type=MESH,
         )
 
-    for load in loads:
+    for load in loads[:-1]:
         load.wait()
+    for load in record_loads[1:] + loads[-1:]:
+        load.start()
     pl.semaphore_wait(barrier, 5)
 
     def whiten_chunk(chunk, carry):
@@ -172,6 +172,7 @@
     whiten_chunk(0, 0)
     transform(1, chunks - 1)
     lax.fori_loop(1, chunks, whiten_chunk, 0)
+    loads[-1].wait()
 
     def cross_lags(blocks, between):
         count = len(blocks)
@@ -225,12 +226,15 @@
             return lax.fori_loop(0, channels // batch, channel_step, carry)
 
         lax.fori_loop(0, tiles, tile_step, 0)
+        depth = channels * GROUP
+        crossed = cross[:count].reshape(count * depth, 2 * BAND)
+        result = jnp.dot(crossed, inverse[...], preferred_element_type=jnp.float32) * norm_factor
         for p, (_, _, step) in enumerate(blocks):
-            result = jnp.dot(cross[p], inverse[...], preferred_element_type=jnp.float32)
-            result = result * norm_factor
             for part in range(n_hour):
                 lanes = slice(part * quarter, (part + 1) * quarter)
-                lagged[step, part % 2, part // 2] = result[:, lanes].astype(jnp.bfloat16)
+                lagged[step, part % 2, part // 2] = result[
+                    p * depth : (p + 1) * depth, lanes
+                ].astype(jnp.bfloat16)
             to_core(step).start()
 
     def relay(step):

time: 55.1 us -> 53.9 us (0.978)
  Pallas kernels: 52.8 us -> 51.7 us
    pallas_call x1, Pallas kernels: 52.8 us -> 51.7 us  [local(): pl.pallas_call(functools.partial(kernel, n_chan, n_hour, channels, window...]
where the time goes in v5:
time: 53.9 us; the launch traced here: 53.8 us
  Pallas kernels  51.7 us (96%)
  local copies, waits for them, and re-layouts  2.11 us (4%)
    pallas_call x1, Pallas kernels, local(): pl.pallas_call(functools.partial(kernel, n_chan, n_hour, channels, window...  51.7 us
    unnamed x1, local copies, waits for them, and re-layouts  2.11 us

profile of v5, /device:TPU:0, one launch (start us, length us, event | category | flops | bytes accessed | tf_op | source)
XLA Modules:
  0.0 53.8 jit_solution(16957038423721570537)
XLA Ops:
  0.0 51.7 %correlate.1 = bf16[40,2,40,128]{3,2,1,0:T(8,128)(2,1)} custom-call(bf16[640,2048]{1,0:T(8,128)(2,1)} %bitcast.3, s32[1,40]{1,0:T(1,128)} %bitcast.4, s32[1,16]{1,0:T(1,128)} %bitcast.5, bf16[2048,1024]{1,0:T(8,128)(2,1)} %constant.8.clone.forward_hbm, bf16[512,512]{1,0:T(8,128)(2,1)} %constant.9.clone.inside_hbm, f32[1,512]{1,0:T(1,128)} %constant.10.clone.weight_hbm, ...), custom_call_target="tpu_custom_call" | custom-call | tf_op jit(solution)/shard_map/correlate/pallas_call | solution.py:308
  51.7 2.1 %copy.9 = bf16[40,2,40,128]{3,2,1,0:T(8,128)(2,1)} copy(bf16[40,2,40,128]{3,2,1,0:T(8,128)(2,1)} %correlate.1) | data formatting | bytes 1638400
